TPU v7x, 32 devices: a whole 2x2x4 slice. The times are simulated.
32 devices in a mesh: fsdp: 32 (over z, y, x, core).
Axes of the slice: x: 2, y: 2, z: 4, core: 2. Of those that a mesh axis runs over, the one named last changes fastest.
Arguments:
- tokens: bfloat16 [65536, 768], P('fsdp'), may hold values from -6 to 6
- mol_len: int32 [256], P('fsdp'), may hold values from 0 to 256, as said below
- cotangent: bfloat16 [65536, 768], P('fsdp'), may hold values from -6 to 6
- ln1_gain: bfloat16 [768], P('fsdp'), may hold values from 0.5 to 1.5
- ln1_bias: bfloat16 [768], P('fsdp'), may hold values from -1 to 1
- w_qkv: bfloat16 [768, 2304], P('fsdp'), may hold values from -0.21875 to 0.21875
- q_bias: bfloat16 [768], P('fsdp'), may hold values from -1 to 1
- v_bias: bfloat16 [768], P('fsdp'), may hold values from -1 to 1
- w_out: bfloat16 [768, 768], P('fsdp'), may hold values from -1.25 to 1.25
- out_bias: bfloat16 [768], P('fsdp'), may hold values from -1 to 1
- ln2_gain: bfloat16 [768], P('fsdp'), may hold values from 0.5 to 1.5
- ln2_bias: bfloat16 [768], P('fsdp'), may hold values from -1 to 1
- w_in: bfloat16 [768, 768], P('fsdp'), may hold values from -0.21875 to 0.21875
- in_bias: bfloat16 [768], P('fsdp'), may hold values from -1 to 1
- w_back: bfloat16 [768, 768], P('fsdp'), may hold values from -0.21875 to 0.21875
- back_bias: bfloat16 [768], P('fsdp'), may hold values from -1 to 1
Outputs:
- mixed_out: bfloat16 [65536, 768], P('fsdp')
- token_grad: bfloat16 [65536, 768], P('fsdp')
- grad_ln1_gain: float32 [768], P('fsdp')
- grad_ln1_bias: float32 [768], P('fsdp')
- grad_w_qkv: float32 [768, 2304], P('fsdp')
- grad_q_bias: float32 [768], P('fsdp')
- grad_v_bias: float32 [768], P('fsdp')
- grad_w_out: float32 [768, 768], P('fsdp')
- grad_out_bias: float32 [768], P('fsdp')
- grad_ln2_gain: float32 [768], P('fsdp')
- grad_ln2_bias: float32 [768], P('fsdp')
- grad_w_in: float32 [768, 768], P('fsdp')
- grad_in_bias: float32 [768], P('fsdp')
- grad_w_back: float32 [768, 768], P('fsdp')
- grad_back_bias: float32 [768], P('fsdp')
Inputs may be any that keep to these rules, and one draw needn't show every extreme that they name: `mol_len`: each slot of 256 tokens holds one molecule or is empty; the first slot of every device is used; on one device every slot is used and one slot is full, on another only the first is used.
All inputs are finite; a program needn't handle non-finite values.
Results may differ from a plain program's by a relative error of at most 0.012.
Values may be sent and summed in bfloat16 or wider, within the bound.
A program may use at most 192 MiB of HBM per device.

v0:
```python
import functools

import jax
import jax.numpy as jnp
from jax import lax
from jax.experimental import pallas as pl
from jax.experimental.pallas import tpu as pltpu
from jax.sharding import PartitionSpec as P

HEADS = 32

bf16 = jnp.bfloat16
f32 = jnp.float32
eps = 1e-05
masked_score = -1e30
log2_e = 1.4426950408889634
MESH = pl.DeviceIdType.MESH
MIB = 1 << 20

PLANES = 4
CHIPS = 4 * PLANES
DEVICES = 2 * CHIPS
SHARD = 24
VECTORS = 9
COPIES = 8


def dot(left, right, left_dim, right_dim):
    return lax.dot_general(
        left, right, (((left_dim,), (right_dim,)), ((), ())), preferred_element_type=f32
    )


def normalize(values):
    centred = values - jnp.mean(values, axis=-1, keepdims=True)
    factor = lax.rsqrt(jnp.mean(centred * centred, axis=-1, keepdims=True) + eps)
    return centred * factor, factor


def norm_backward(d_normed, gain, unit, factor):
    e = d_normed * gain
    inner = jnp.mean(e * unit, axis=-1, keepdims=True)
    return factor * (e - jnp.mean(e, axis=-1, keepdims=True) - unit * inner)


def fold_rows(values):
    rows, columns = values.shape
    return jnp.sum(values.reshape(rows // 8, 8, columns), axis=0)


class Place:
    def __init__(self):
        me = lax.axis_index("fsdp")
        self.me = me
        self.c = lax.rem(me, 2)
        self.x = lax.rem(me // 2, 2)
        self.y = lax.rem(me // 4, 2)
        self.z = me // 8
        self.sib = me + 1 - 2 * self.c
        self.xn = me + 2 - 4 * self.x
        self.yn = me + 4 - 8 * self.y

    def block(self, c, z, y, x):
        return ((c * PLANES + z) * 2 + y) * 2 + x

    def greet(self):
        sem = pltpu.get_barrier_semaphore()

        def signal(device):
            pl.semaphore_signal(sem, inc=1, device_id=(device,), device_id_type=MESH)

        for device in (self.sib, self.xn, self.yn):
            signal(device)
        for distance in range(1, PLANES):
            signal(lax.rem(self.me + 8 * distance, DEVICES))

    def await_all(self):
        pl.semaphore_wait(pltpu.get_barrier_semaphore(), 2 + PLANES)


def gather_kernel(
    len_ref,
    *refs,
):
    lines, refs = refs[:VECTORS], refs[VECTORS:]
    gather_body(len_ref, lines, *refs)


def gather_body(
    len_ref,
    lines,
    wq_ref,
    wo_ref,
    wi_ref,
    wb_ref,
    tok_ref,
    cot_hbm,
    qkv_hbm,
    unit_hbm,
    fq_hbm,
    fo_hbm,
    fi_hbm,
    fb_hbm,
    tok_hbm,
    cot_out,
    vec_ref,
    work_ref,
    gq,
    gr,
    fq,
    fo,
    fi,
    fb,
    fq_t,
    unit,
    unit_t,
    qkv,
    bias,
    tok_odd,
    cot_odd,
    len_send,
    len_recv,
    send_sem,
    recv_sem,
    swap_send,
    swap_recv,
    copy_sem,
):
    at = Place()
    at.greet()
    width = tok_ref.shape[1]
    slots, _, block = qkv.shape
    shared = slots // 2
    half_q = 3 * width // 2
    half = width // 2
    own = at.block(at.c, at.z, at.y, at.x)
    mine, theirs = at.c * CHIPS, (1 - at.c) * CHIPS
    slabs = ((gq, 0, 384), (gq, 384, 384), (gq, 768, 512), (gr, 0, 640), (gr, 640, 512))

    small = [line[...].astype(f32).reshape(1, SHARD) for line in lines]
    small = jnp.concatenate(small + [jnp.zeros((2 * SHARD - VECTORS, SHARD), f32)], axis=0)
    small = jnp.concatenate([small, jnp.zeros((2 * SHARD, 128 - SHARD), f32)], axis=1).astype(bf16)
    gq[own] = jnp.concatenate(
        [
            jnp.concatenate([wq_ref[:, :half_q], wq_ref[:, half_q:]], axis=0),
            small,
        ],
        axis=1,
    )
    gr[own] = jnp.concatenate(
        [
            jnp.concatenate([wo_ref[...], wi_ref[...]], axis=0),
            jnp.concatenate([wb_ref[:, :half], wb_ref[:, half:]], axis=0),
        ],
        axis=1,
    )

    def view(k, first, count):
        slab, column, columns = slabs[k]
        return slab.at[pl.ds(first, count), :, pl.ds(column, columns)]

    def remote(k, first, target, sem, count=1):
        return pltpu.make_async_remote_copy(
            src_ref=view(k, first, count),
            dst_ref=view(k, first, count),
            send_sem=send_sem.at[k],
            recv_sem=recv_sem.at[k, sem],
            device_id=(target,),
            device_id_type=MESH,
        )

    def send(k, b, target):
        remote(k, b, target, lax.rem(b, CHIPS)).start()

    def to_sib(k, b):
        remote(k, b, at.sib, CHIPS).start()

    def arrived(k, b):
        remote(k, b, at.sib, lax.rem(b, CHIPS)).wait_recv()

    def at_level(shift, body):
        level = at.z + shift
        if shift == 0:
            body(level)
        else:
            pl.when((level >= 0) & (level <= PLANES - 1))(lambda: body(level))

    def both(s):
        return (0,) if s == 0 else (-s, s)

    def own_plane(k):
        send(k, own, at.xn)
        send(k, own, at.yn)

    def own_column(k):
        for s in range(1, PLANES):
            for shift in both(s):
                at_level(shift, lambda level, shift=shift: send(k, own, at.me + 8 * shift))
        to_sib(k, own)

    def column(k, s):
        def body(level):
            b = at.block(at.c, level, at.y, at.x)
            arrived(k, b)
            send(k, b, at.xn)
            send(k, b, at.yn)
            to_sib(k, b)

        for shift in both(s):
            at_level(shift, body)

    def plane(k, s):
        def body(level):
            even = lax.rem(level, 2) == 0
            b = at.block(at.c, level, at.y, 1 - at.x)
            arrived(k, b)
            pl.when(even)(lambda: send(k, b, at.yn))
            to_sib(k, b)
            d = at.block(at.c, level, 1 - at.y, at.x)
            arrived(k, d)
            pl.when(jnp.logical_not(even))(lambda: send(k, d, at.xn))
            to_sib(k, d)

        for shift in both(s):
            at_level(shift, body)

    def corner(k):
        for j in range(PLANES):
            b = at.block(at.c, j, 1 - at.y, 1 - at.x)
            arrived(k, b)
            to_sib(k, b)

    def others(k):
        remote(k, theirs, at.sib, CHIPS, CHIPS).wait_recv()

    def rows_of(i):
        return pl.ds(i * block, block)

    cot_in = [
        pltpu.make_async_copy(
            cot_hbm.at[rows_of(2 * i + 1)], cot_odd.at[rows_of(i)], swap_recv.at[6 + i]
        )
        for i in range(shared)
    ]

    def swap_copy(src, dst, send, recv):
        return pltpu.make_async_remote_copy(
            src_ref=src,
            dst_ref=dst,
            send_sem=swap_send.at[send],
            recv_sem=swap_recv.at[recv],
            device_id=(at.sib,),
            device_id_type=MESH,
        )

    def tok_copy(i):
        return swap_copy(tok_ref.at[rows_of(2 * i + 1)], tok_odd.at[rows_of(i)], 0, i)

    def swap_start():
        swap_copy(len_send, len_recv, 2, 5).start()
        for i in range(shared):
            tok_copy(i).start()
        for i in range(shared):
            cot_in[i].wait()
            swap_copy(cot_odd.at[rows_of(i)], cot_out.at[rows_of(i)], 1, 4).start()

    def swap_end():
        swap_copy(len_send, len_recv, 2, 5).wait()
        swap_copy(tok_odd, tok_odd, 0, 0).wait_send()
        swap_copy(cot_odd, cot_out, 1, 4).wait()
        place = lax.broadcasted_iota(jnp.int32, (shared, 128), 0)
        own_lengths = jnp.zeros((shared, 128), jnp.int32)
        odd_lengths = jnp.zeros((shared, 128), jnp.int32)
        for i in range(shared):
            own_lengths = jnp.where(place == i, len_send[2 * i : 2 * i + 1], own_lengths)
            odd_lengths = jnp.where(place == i, len_recv[2 * i + 1 : 2 * i + 2], odd_lengths)
        work_ref[:shared] = own_lengths
        work_ref[shared:] = odd_lengths

    for i in range(slots):
        len_send[i : i + 1] = jnp.full((1, 128), len_ref[i], jnp.int32)
    for copy in cot_in:
        copy.start()

    def norm_step(m):
        rows = rows_of(m)
        if m < shared:
            here = tok_ref[rows_of(2 * m)]
        else:
            tok_copy(m - shared).wait_recv()
            here = tok_odd[rows_of(m - shared)]
        size = block // 2
        for i in range(2):
            some = pl.ds(m * block + i * size, size)
            values, _ = normalize(here[i * size : (i + 1) * size].astype(f32))
            unit[some] = values
            unit_t[:, some] = values.astype(bf16).T

    def strip(i):
        return pl.ds(pl.multiple_of(i * 2 * SHARD, 2 * SHARD), 2 * SHARD)

    def stack(first, second):
        return jnp.concatenate([first, second], axis=0).astype(bf16)

    def build_q():
        def body(i, carry):
            first = gq[i].astype(f32)
            second = gq[CHIPS + i].astype(f32)
            fq[strip(i), :half_q] = stack(first[:SHARD, :half_q], second[:SHARD, :half_q])
            fq[strip(i), half_q:] = stack(first[SHARD:, :half_q], second[SHARD:, :half_q])
            return carry

        lax.fori_loop(0, CHIPS, body, 0)
        out(fq, fq_hbm)

    def build_r():
        def body(i, carry):
            first = gr[i].astype(f32)
            second = gr[CHIPS + i].astype(f32)
            fo[strip(i)] = stack(first[:SHARD, :width], second[:SHARD, :width])
            fi[strip(i)] = stack(first[SHARD:, :width], second[SHARD:, :width])
            fb[strip(i), :half] = stack(first[:SHARD, width:], second[:SHARD, width:])
            fb[strip(i), half:] = stack(first[SHARD:, width:], second[SHARD:, width:])
            return carry

        lax.fori_loop(0, CHIPS, body, 0)
        out(fo, fo_hbm)
        out(fi, fi_hbm)
        out(fb, fb_hbm)

    copies = []

    def out(src, dst):
        copy = pltpu.make_async_copy(src, dst, copy_sem.at[len(copies)])
        copy.start()
        copies.append(copy)

    def turn(part):
        columns = slice(part * width, (part + 1) * width)
        fq_t[columns] = fq[:, columns].T

    def spread_vectors():
        column_at = lax.broadcasted_iota(jnp.int32, (128, width), 1)
        entry = lax.broadcasted_iota(jnp.int32, (128, width), 0)
        spread = jnp.where(lax.rem(column_at, SHARD) == entry, 1.0, 0.0).astype(bf16)
        stacked = jnp.concatenate([gq[p, :16, half_q:] for p in range(DEVICES)], axis=0)
        wide = dot(stacked, spread, 1, 0)
        total = jnp.zeros((16, width), f32)
        column_at = lax.broadcasted_iota(jnp.int32, (16, width), 1)
        for p in range(DEVICES):
            first = SHARD * ((p % CHIPS) * 2 + p // CHIPS)
            here = (column_at >= first) & (column_at < first + SHARD)
            total = total + jnp.where(here, wide[16 * p : 16 * p + 16], 0.0)
        vec_ref[...] = total
        bias[:width] = jnp.broadcast_to(total[2:3], (128, width)).T
        bias[width : 2 * width] = jnp.zeros((width, 128), f32)
        bias[2 * width :] = jnp.broadcast_to(total[3:4], (128, width)).T

    def qkv_copy(m):
        return pltpu.make_async_copy(qkv.at[m], qkv_hbm.at[m], copy_sem.at[COPIES + m])

    def qkv_part(m, part):
        here = unit[pl.ds(pl.multiple_of(m * block, block), block)]
        normed = (here * vec_ref[0:1] + vec_ref[1:2]).astype(bf16)
        lines = pl.ds(pl.multiple_of(part * width, width), width)
        result = dot(fq_t[lines], normed, 1, 1)
        added = jnp.concatenate([bias[lines]] * (block // 128), axis=1)
        qkv[m, lines] = (result + added).astype(bf16)
        pl.when(part == 2)(lambda: qkv_copy(m).start())

    norm_step(0)
    norm_step(1)
    at.await_all()
    swap_start()
    own_column(0)
    own_column(1)
    own_plane(1)
    own_plane(2)
    norm_step(2)
    own_plane(4)
    own_plane(3)
    own_column(2)
    own_plane(0)
    column(0, 3)
    column(0, 2)
    plane(1, 0)
    column(0, 1)
    plane(0, 3)
    plane(0, 0)
    own_column(3)
    column(1, 3)
    own_column(4)
    column(1, 1)
    norm_step(3)
    norm_step(4)
    column(1, 2)
    plane(2, 0)
    plane(0, 1)
    plane(1, 3)
    norm_step(5)
    norm_step(6)
    column(2, 3)
    column(2, 1)
    column(2, 2)
    plane(1, 2)
    plane(1, 1)
    norm_step(7)
    plane(0, 2)
    plane(2, 1)
    plane(2, 3)
    plane(2, 2)
    corner(1)
    column(3, 3)
    corner(0)
    plane(3, 0)
    corner(2)
    column(3, 2)
    others(1)
    others(0)
    plane(4, 0)
    column(3, 1)
    others(2)
    column(4, 3)
    build_q()
    plane(3, 3)
    column(4, 1)
    turn(0)
    turn(1)
    turn(2)
    spread_vectors()
    column(4, 2)

    def beside_qkv_6():
        plane(3, 2)

    def beside_qkv_7():
        plane(3, 1)

    def beside_qkv_8():
        plane(4, 1)

    def beside_qkv_11():
        plane(4, 2)
        plane(4, 3)

    def beside_qkv_14():
        corner(3)

    def beside_qkv_19():
        corner(4)

    def beside_qkv_22():
        others(4)
        others(3)


    def beside_qkv_step(i, carry):
        qkv_part(i // 3, lax.rem(i, 3))
        pl.when(i == 6)(beside_qkv_6)
        pl.when(i == 7)(beside_qkv_7)
        pl.when(i == 8)(beside_qkv_8)
        pl.when(i == 11)(beside_qkv_11)
        pl.when(i == 14)(beside_qkv_14)
        pl.when(i == 19)(beside_qkv_19)
        pl.when(i == 22)(beside_qkv_22)
        return carry

    lax.fori_loop(0, 24, beside_qkv_step, 0)
    build_r()
    out(unit_t, unit_hbm)
    out(tok_odd, tok_hbm)
    swap_end()
    for k in range(len(slabs)):
        remote(k, 0, at.sib, 0, DEVICES - 1).wait_send()
    for copy in copies:
        copy.wait()
    for m in range(slots):
        qkv_copy(m).wait()


def gather_and_project(mol_len, vectors, w_qkv, w_out, w_in, w_back, tokens, cotangent):
    slots = mol_len.shape[0]
    rows, width = tokens.shape
    block = rows // slots
    wide = 3 * width
    vmem = pl.BlockSpec(memory_space=pltpu.VMEM)
    anywhere = pl.BlockSpec(memory_space=pl.ANY)
    square = (width, width)
    return pl.pallas_call(
        gather_kernel,
        out_shape=[
            jax.ShapeDtypeStruct((slots, wide, block), bf16),
            jax.ShapeDtypeStruct((width, rows), bf16),
            jax.ShapeDtypeStruct((width, wide), bf16),
            jax.ShapeDtypeStruct(square, bf16),
            jax.ShapeDtypeStruct(square, bf16),
            jax.ShapeDtypeStruct(square, bf16),
            jax.ShapeDtypeStruct((rows // 2, width), bf16),
            jax.ShapeDtypeStruct((rows // 2, width), bf16),
            jax.ShapeDtypeStruct((16, width), f32),
            jax.ShapeDtypeStruct((slots, 128), jnp.int32),
        ],
        in_specs=[pl.BlockSpec(memory_space=pltpu.SMEM)] + [vmem] * (VECTORS + 5) + [anywhere],
        out_specs=[anywhere] * 8 + [vmem] * 2,
        scratch_shapes=[
            pltpu.VMEM((DEVICES, 2 * SHARD, wide // 2 + 128), bf16),
            pltpu.VMEM((DEVICES, 2 * SHARD, wide // 2), bf16),
            pltpu.VMEM((width, wide), bf16),
            pltpu.VMEM(square, bf16),
            pltpu.VMEM(square, bf16),
            pltpu.VMEM(square, bf16),
            pltpu.VMEM((wide, width), bf16),
            pltpu.VMEM((rows, width), f32),
            pltpu.VMEM((width, rows), bf16),
            pltpu.VMEM((slots, wide, block), bf16),
            pltpu.VMEM((wide, 128), f32),
            pltpu.VMEM((rows // 2, width), bf16),
            pltpu.VMEM((rows // 2, width), bf16),
            pltpu.VMEM((slots, 128), jnp.int32),
            pltpu.VMEM((slots, 128), jnp.int32),
            pltpu.SemaphoreType.DMA((5,)),
            pltpu.SemaphoreType.DMA((5, CHIPS + 1)),
            pltpu.SemaphoreType.DMA((3,)),
            pltpu.SemaphoreType.DMA((6 + slots // 2,)),
            pltpu.SemaphoreType.DMA((COPIES + slots,)),
        ],
        compiler_params=pltpu.CompilerParams(
            collective_id=0, has_side_effects=True, vmem_limit_bytes=60 * MIB
        ),
    )(mol_len, *vectors, w_qkv, w_out, w_in, w_back, tokens, cotangent)


def middle_kernel(
    packed,
    head_dim,
    len_ref,
    qkv_ref,
    tok_first,
    tok_second,
    cot_first,
    cot_second,
    wout_ref,
    win_ref,
    wback_ref,
    vec_ref,
    mixed_out,
    dmix_ref,
    dqkv_ref,
    gvec_ref,
    *rest,
):
    if packed:
        mixed_odd, packed_ref, gout_ref, gin_ref, gback_ref, *rest = rest
    else:
        gout_ref, gin_ref, gback_ref, *rest = rest
    probs, ctx_s, linv_s, dctx_s, tok_ref, cot_ref, mixed_ref = rest
    step = pl.program_id(0)
    block, width = tok_ref.shape
    slot = 32
    group = 4
    heads = width // head_dim
    span = group * head_dim
    scale = head_dim ** (-0.5)
    length = len_ref[step, 0]
    first = step < pl.num_programs(0) // 2
    tok_ref[...] = jnp.where(first, tok_first[...], tok_second[...])
    cot_ref[...] = jnp.where(first, cot_first[...], cot_second[...])

    @pl.when(step == 0)
    def _():
        gout_ref[...] = jnp.zeros_like(gout_ref)
        gin_ref[...] = jnp.zeros_like(gin_ref)
        gback_ref[...] = jnp.zeros_like(gback_ref)
        gvec_ref[...] = jnp.zeros_like(gvec_ref)

    def run(size, keys):
        extra = (slot - head_dim, size)
        sub = lax.broadcasted_iota(jnp.int32, extra, 0)
        lane = lax.broadcasted_iota(jnp.int32, extra, 1)
        one_row = jnp.where(sub == 0, 1.0, 0.0).astype(f32)
        two_rows = jnp.where(sub <= 1, 1.0, 0.0).astype(f32)
        mask_row = jnp.where((sub == 0) & (lane >= length), masked_score, 0.0).astype(f32)

        def group_rows(base, g):
            return slice(base + g * span, base + (g + 1) * span)

        def load(base, g):
            return qkv_ref[group_rows(base, g), :size].astype(f32)

        def place(j, rows):
            parts = []
            if j > 0:
                parts.append(jnp.zeros((slot * j, size), bf16))
            parts.append(rows)
            if j < group - 1:
                parts.append(jnp.zeros((slot * (group - 1 - j), size), bf16))
            return jnp.concatenate(parts, axis=0)

        def pieces(values):
            return [values[head_dim * j : head_dim * (j + 1)] for j in range(group)]

        def padded(values, tail):
            return [jnp.concatenate([p, tail], axis=0).astype(bf16) for p in pieces(values)]

        together = 1 if size == block else 2
        units = heads // together
        ahead = 3 if size == block else 6

        def beside(parts):
            return parts[0] if together == 1 else jnp.concatenate(parts, axis=1)

        def below(parts):
            return parts[0] if together == 1 else jnp.concatenate(parts, axis=0)

        def stacked(pair):
            return below([pair[:, i * size : (i + 1) * size] for i in range(together)])

        def own_part(value, i, n):
            return value[slot * i : slot * i + head_dim, i * n : (i + 1) * n]

        def all_keys(value):
            if keys == size:
                return value
            return jnp.concatenate([value, jnp.zeros((value.shape[0], size - keys), f32)], axis=1)

        def members(u):
            g, first = divmod(u * together, group)
            return g, range(first, first + together)

        def forward():
            q, k, v, scores, weights, outs = {}, {}, {}, {}, {}, {}
            for t in range(units + 2 * ahead):
                if t < units:
                    g, js = members(t)
                    if js[0] == 0:
                        q[g] = padded(load(0, g), one_row)
                        k[g] = jnp.concatenate(padded(load(width, g), mask_row), axis=0).T[:keys]
                        v[g] = padded(load(2 * width, g), one_row)
                    scores[t] = dot(k[g], beside([place(j, q[g][j]) for j in js]), 1, 0)
                u = t - ahead
                if 0 <= u < units:
                    s = scores.pop(u)
                    peak = jnp.max(s, axis=0, keepdims=True)
                    weights[u] = jnp.exp2((s - peak) * (scale * log2_e)).astype(bf16)
                    probs[u, :keys, : together * size] = weights[u]
                u = t - 2 * ahead
                if 0 <= u < units:
                    g, js = members(u)
                    o = dot(below([v[g][j] for j in js])[:, :keys], weights.pop(u), 1, 0)
                    for i, j in enumerate(js):
                        total = slot * i + head_dim
                        inverse = 1.0 / o[total : total + 1, i * size : (i + 1) * size]
                        linv_s[g * group + j, :, :size] = jnp.broadcast_to(inverse, (8, size))
                        outs[j] = own_part(o, i, size) * inverse
                    if js[-1] == group - 1:
                        parts = [outs.pop(j) for j in range(group)]
                        ctx_s[group_rows(0, g), :size] = jnp.concatenate(parts, axis=0)

        forward()

        live = (lax.broadcasted_iota(jnp.int32, (keys, 1), 0) < length).astype(f32)
        out_bias, gain, shift = vec_ref[4:5], vec_ref[5:6], vec_ref[6:7]
        in_bias, back_bias = vec_ref[7:8], vec_ref[8:9]

        strips = [slice(c, c + 256) for c in range(0, width, 256)]

        def row_mean(parts):
            return sum(jnp.sum(p, axis=1, keepdims=True) for p in parts) * (1.0 / width)

        def join(parts):
            return jnp.concatenate(parts, axis=1)

        d_ffn = cot_ref[:keys].astype(f32) * live
        gvec_ref[4] += fold_rows(d_ffn)
        d_ffn = d_ffn.astype(bf16)
        ctx_t = ctx_s[:, :size].astype(bf16)
        ctx = ctx_t.T[:keys]
        mixed = []
        for c in strips:
            attn = dot(ctx, wout_ref[:, c], 1, 0) + out_bias[:, c]
            mixed.append(tok_ref[:keys, c].astype(f32) + live * attn)
        d_act = [dot(d_ffn, wback_ref[c], 1, 1) for c in strips[:1]]
        mean = row_mean(mixed)
        centred = [m - mean for m in mixed]
        factor = lax.rsqrt(row_mean([v * v for v in centred]) + eps)
        unit = [v * factor for v in centred]
        normed = join(
            [(u * gain[:, c] + shift[:, c]).astype(bf16) for u, c in zip(unit, strips)]
        )
        act, d_pre = [], []

        def project(c):
            return dot(normed, win_ref[:, c], 1, 0) + in_bias[:, c]

        ahead_pre = [project(strips[0])]
        for i, c in enumerate(strips):
            if i + 1 < len(strips):
                ahead_pre.append(project(strips[i + 1]))
                d_act.append(dot(d_ffn, wback_ref[strips[i + 1]], 1, 1))
            pre = ahead_pre[i]
            cdf = 0.5 * (1.0 + lax.erf(pre * 0.7071067811865476))
            act.append((pre * cdf).astype(bf16))
            slope = cdf + pre * jnp.exp(-0.5 * pre * pre) * 0.3989422804014327
            low = (d_act[i] * slope).astype(bf16)
            gvec_ref[3, :, c] += fold_rows(low.astype(f32))
            d_pre.append(low)
        act, d_pre = join(act), join(d_pre)
        d_normed = [dot(d_pre, win_ref[c], 1, 1) for c in strips]
        for m, c in zip(mixed, strips):
            branch = dot(act, wback_ref[:, c], 1, 0) + back_bias[:, c]
            mixed_ref[:keys, c] = (m + live * branch).astype(bf16)
        act_t, normed_t = act.T, normed.T
        e = []
        for i, c in enumerate(strips):
            gback_ref[:, c] += dot(act_t, d_ffn[:, c], 1, 0)
            gvec_ref[1, :, c] += fold_rows(d_normed[i] * unit[i])
            gvec_ref[2, :, c] += fold_rows(d_normed[i])
            e.append(d_normed[i] * gain[:, c])
        mean = row_mean(e)
        inner = row_mean([v * u for v, u in zip(e, unit)])
        d_attn = []
        for i, c in enumerate(strips):
            gin_ref[:, c] += dot(normed_t, d_pre[:, c], 1, 0)
            d_mixed = cot_ref[:keys, c].astype(f32) + factor * (e[i] - mean - unit[i] * inner)
            dmix_ref[:keys, c] = d_mixed
            low = (live * d_mixed).astype(bf16)
            gvec_ref[0, :, c] += fold_rows(low.astype(f32))
            d_attn.append(low)
        d_attn = join(d_attn)
        for c in strips:
            d_ctx = dot(wout_ref[c], d_attn, 1, 1)
            dctx_s[c, :size] = all_keys(d_ctx).astype(bf16)
        for c in strips:
            gout_ref[:, c] += dot(ctx_t[:, :keys], d_attn[:, c], 1, 0)

        behind = 3 if size == block else 4

        def backward():
            q, k, v, d, d_probs, d_scores = {}, {}, {}, {}, {}, {}
            d_q, d_k, d_v = {}, {}, {}
            for t in range(units + 2 * behind):
                if t < units:
                    g, js = members(t)
                    if js[0] == 0:
                        q[g] = padded(load(0, g), one_row)
                        k[g] = padded(load(width, g), one_row)
                        v[g] = jnp.concatenate(padded(load(2 * width, g), two_rows), axis=0).T[:keys]
                        d_out = pieces(dctx_s[group_rows(0, g), :size].astype(f32))
                        out = pieces(ctx_s[group_rows(0, g), :size])
                        d[g] = []
                        for i in range(group):
                            scaled = d_out[i] * linv_s[g * group + i, :1, :size]
                            inner = -jnp.sum(scaled * out[i], axis=0, keepdims=True)
                            high = inner.astype(bf16).astype(f32)
                            blank = jnp.zeros((slot - head_dim - 2, size), f32)
                            tail = [scaled, high, inner - high, blank]
                            d[g].append(jnp.concatenate(tail, axis=0).astype(bf16))
                    d_probs[t] = dot(v[g], beside([place(j, d[g][j]) for j in js]), 1, 0)
                u = t - behind
                if 0 <= u < units:
                    p = probs[u, :keys, : together * size]
                    d_scores[u] = (p.astype(f32) * d_probs.pop(u)).astype(bf16)
                u = t - 2 * behind
                if 0 <= u < units:
                    g, js = members(u)
                    ds = d_scores.pop(u)
                    p = stacked(probs[u, :keys, : together * size])
                    to_v = dot(below([d[g][j] for j in js]), p, 1, 1)
                    to_q = dot(below([k[g][j] for j in js])[:, :keys], ds, 1, 0)
                    to_k = dot(below([q[g][j] for j in js]), stacked(ds), 1, 1)
                    for i, j in enumerate(js):
                        d_v[j] = all_keys(own_part(to_v, i, keys))
                        d_q[j] = own_part(to_q, i, size) * scale
                        d_k[j] = all_keys(own_part(to_k, i, keys) * scale)
                    if js[-1] == group - 1:
                        for base, parts in ((0, d_q), (width, d_k), (2 * width, d_v)):
                            some = [parts.pop(j) for j in range(group)]
                            dqkv_ref[group_rows(base, g), :size] = jnp.concatenate(
                                some, axis=0
                            ).astype(bf16)

        backward()

        if keys < block:
            mixed_ref[keys:] = tok_ref[keys:]
            dmix_ref[keys:] = cot_ref[keys:].astype(f32)
        if size < block:
            dqkv_ref[:, size:] = jnp.zeros((3 * width, block - size), bf16)

    half = block // 2

    @pl.when(length == 0)
    def _():
        mixed_ref[...] = tok_ref[...]
        dmix_ref[...] = cot_ref[...].astype(f32)
        dqkv_ref[...] = jnp.zeros_like(dqkv_ref)

    @pl.when((length > 0) & (length <= half))
    def _():
        run(half, half)

    more = half + half // 2

    @pl.when((length > half) & (length <= more))
    def _():
        run(block, more)

    @pl.when(length > more)
    def _():
        run(block, block)

    if packed:

        @pl.when(first)
        def _():
            mixed_out[...] = mixed_ref[...]

        @pl.when(jnp.logical_not(first))
        def _():
            mixed_odd[...] = mixed_ref[...]

    else:
        mixed_out[...] = mixed_ref[...]

    if packed:

        @pl.when(step == pl.num_programs(0) - 1)
        def _():
            columns = width // 2
            for i in range(DEVICES):
                p = (i % 2) * CHIPS + i // 2
                rows = slice(SHARD * i, SHARD * (i + 1))
                top = jnp.concatenate([gout_ref[rows], gback_ref[rows, :columns]], axis=1)
                bottom = jnp.concatenate([gin_ref[rows], gback_ref[rows, columns:]], axis=1)
                packed_ref[p] = jnp.concatenate([top, bottom], axis=0).astype(bf16)


def middle(lengths, qkv, tokens, cotangent, w_out, w_in, w_back, vectors, packed):
    slots, wide, block = qkv.shape
    rows, width = slots * block, wide // 3
    square = (width, width)
    shared = slots // 2

    def whole(shape):
        return pl.BlockSpec(shape, lambda m: (0,) * len(shape))

    by_rows = pl.BlockSpec((block, width), lambda m: (m, 0))
    if packed:
        first = pl.BlockSpec((block, width), lambda m: (2 * jnp.minimum(m, shared - 1), 0))
        second = pl.BlockSpec((block, width), lambda m: (jnp.maximum(m - shared, 0), 0))
    else:
        first = pl.BlockSpec((block, width), lambda m: (jnp.minimum(m, shared - 1), 0))
        second = pl.BlockSpec((block, width), lambda m: (jnp.maximum(m, shared), 0))
    out_specs = [
        by_rows,
        by_rows,
        pl.BlockSpec((3 * width, block), lambda m: (0, m)),
        whole((5, 8, width)),
    ]
    out_shape = [
        jax.ShapeDtypeStruct((rows, width), bf16),
        jax.ShapeDtypeStruct((rows, width), f32),
        jax.ShapeDtypeStruct((3 * width, rows), bf16),
        jax.ShapeDtypeStruct((5, 8, width), f32),
    ]
    scratch = [
        pltpu.VMEM((HEADS, block, block), bf16),
        pltpu.VMEM((width, block), f32),
        pltpu.VMEM((HEADS, 8, block), f32),
        pltpu.VMEM((width, block), bf16),
        pltpu.VMEM((block, width), bf16),
        pltpu.VMEM((block, width), bf16),
        pltpu.VMEM((block, width), bf16),
    ]
    if packed:
        shape = (DEVICES, 2 * SHARD, width + width // 2)
        out_specs[0] = first
        out_specs += [second, whole(shape)]
        out_shape.append(jax.ShapeDtypeStruct((rows // 2, width), bf16))
        out_shape.append(jax.ShapeDtypeStruct(shape, bf16))
        scratch = [pltpu.VMEM(square, f32)] * 3 + scratch
    else:
        out_specs += [whole(square)] * 3
        out_shape += [jax.ShapeDtypeStruct(square, f32)] * 3
    return pl.pallas_call(
        functools.partial(middle_kernel, packed, width // HEADS),
        grid=(slots,),
        in_specs=[
            pl.BlockSpec(memory_space=pltpu.SMEM),
            pl.BlockSpec((None, 3 * width, block), lambda m: (m, 0, 0)),
            first,
            second,
            first,
            second,
            whole(square),
            whole(square),
            whole(square),
            whole((16, width)),
        ],
        out_specs=out_specs,
        scratch_shapes=scratch,
        out_shape=out_shape,
        compiler_params=pltpu.CompilerParams(vmem_limit_bytes=58 * MIB),
    )(lengths, qkv, *tokens, *cotangent, w_out, w_in, w_back, vectors)


def scatter_kernel(
    sr_hbm,
    dqkv_hbm,
    unit_hbm,
    fq_hbm,
    tok_hbm,
    odd_hbm,
    dmix_hbm,
    mixed_hbm,
    vec_ref,
    gvec_ref,
    grad_hbm,
    grad_out,
    mixed_out,
    gq_ref,
    gr_ref,
    sq,
    sr,
    rq_sib,
    rr_sib,
    rq,
    rr,
    dqkv,
    unit_t,
    fq,
    tok,
    dmix,
    grad,
    mixed,
    gain_wide,
    shift_wide,
    small_wide,
    sums,
    result,
    send_sem,
    recv_sem,
    swap_send,
    swap_recv,
    copy_sem,
):
    at = Place()
    at.greet()
    rows, width = tok.shape
    wide = 3 * width
    half_q = wide // 2
    slots = 8
    block = rows // slots
    mine, theirs = at.c * CHIPS, (1 - at.c) * CHIPS
    own = at.block(at.c, at.z, at.y, at.x)
    level_rows = 8 * SHARD

    def local(src, dst, i):
        copy = pltpu.make_async_copy(src, dst, copy_sem.at[i])
        copy.start()
        return copy

    sr_in = local(sr_hbm, sr, 0)
    unit_in = local(unit_hbm, unit_t, 1)
    parts_in = []
    for part in range(3):
        some = pl.ds(part * width, width)
        parts_in.append(local(dqkv_hbm.at[some], dqkv.at[some], 2 + 2 * part))
        parts_in.append(local(fq_hbm.at[:, some], fq.at[:, some], 3 + 2 * part))

    def part_wait(part):
        for copy in parts_in[2 * part : 2 * part + 2]:
            copy.wait()

    shared = slots // 2

    def rows_of(i, count=1):
        return pl.ds(i * block, count * block)

    mixed_in = local(mixed_hbm, mixed, 8)
    late = [local(dmix_hbm, dmix, 9), local(odd_hbm, tok.at[rows_of(shared, shared)], 10)]
    for i in range(shared):
        late.append(local(tok_hbm.at[rows_of(2 * i)], tok.at[rows_of(i)], 11 + i))

    def swap_copy(src, dst, i):
        return pltpu.make_async_remote_copy(
            src_ref=src,
            dst_ref=dst,
            send_sem=swap_send.at[i],
            recv_sem=swap_recv.at[i],
            device_id=(at.sib,),
            device_id_type=MESH,
        )

    slabs = (
        (sq, rq_sib, rq, 0, 640),
        (sq, rq_sib, rq, 640, 640),
        (sr, rr_sib, rr, 0, 1152),
    )

    def cut(ref, k, first, count):
        return ref.at[pl.ds(first, count), :, pl.ds(slabs[k][3], slabs[k][4])]

    def piece(ref, k, p):
        _, _, _, column, columns = slabs[k]
        return ref[p, :, column : column + columns].astype(f32)

    def put(k, p, value):
        slab, _, _, column, columns = slabs[k]
        slab[p, :, column : column + columns] = value.astype(bf16)

    def remote(k, src, dst, target, sem):
        return pltpu.make_async_remote_copy(
            src_ref=src,
            dst_ref=dst,
            send_sem=send_sem.at[k],
            recv_sem=recv_sem.at[k, sem],
            device_id=(target,),
            device_id_type=MESH,
        )

    def x_type(j):
        return at.block(at.c, j, at.y, 1 - at.x)

    def y_type(j):
        return at.block(at.c, j, 1 - at.y, at.x)

    def corner_type(j):
        return at.block(at.c, j, 1 - at.y, 1 - at.x)

    def column_type(j):
        return at.block(at.c, j, at.y, at.x)

    def sib_copy(k, j):
        src = cut(slabs[k][0], k, theirs + 4 * j, 4)
        return remote(k, src, cut(slabs[k][1], k, 4 * j, 4), at.sib, j)

    def sib_send(k, j):
        sib_copy(k, j).start()

    def step_copy(k, src, slot, target):
        src = cut(slabs[k][0], k, src, 1)
        return remote(k, src, cut(slabs[k][2], k, slot, 1), target, PLANES + slot)

    def x_send(k, j):
        step_copy(k, x_type(j), 4 + j, at.xn).start()

    def y_send(k, j):
        step_copy(k, y_type(j), 8 + j, at.yn).start()

    def sib_add(k, j):
        sib_copy(k, j).wait_recv()

        def body(i, carry):
            p = mine + 4 * j + i
            put(k, p, piece(slabs[k][0], k, p) + piece(slabs[k][1], k, 4 * j + i))
            return carry

        lax.fori_loop(0, 4, body, 0)
        step_copy(k, corner_type(j), j, at.yn if j % 2 == 0 else at.xn).start()
        (y_send if j % 2 == 0 else x_send)(k, j)

    def corner_add(k, j):
        step_copy(k, own, j, at.sib).wait_recv()
        p = x_type(j) if j % 2 == 0 else y_type(j)
        put(k, p, piece(slabs[k][0], k, p) + piece(slabs[k][2], k, j))
        (x_send if j % 2 == 0 else y_send)(k, j)

    def plane_add(k, j):
        p = column_type(j)
        step_copy(k, own, 4 + j, at.sib).wait_recv()
        step_copy(k, own, 8 + j, at.sib).wait_recv()
        received = piece(slabs[k][2], k, 4 + j) + piece(slabs[k][2], k, 8 + j)
        put(k, p, piece(slabs[k][0], k, p) + received)

        @pl.when(at.z != j)
        def _():
            step_copy(k, p, 12 + at.z, at.me + 8 * (j - at.z)).start()

    def land(k):
        total = gq_ref if slabs[k][0] is sq else gr_ref
        columns = slice(slabs[k][3], slabs[k][3] + slabs[k][4])
        total[:, columns] = piece(slabs[k][0], k, own)
        for j in range(PLANES):

            @pl.when(at.z != j)
            def _():
                step_copy(k, own, 12 + j, at.sib).wait_recv()
                total[:, columns] += piece(slabs[k][2], k, 12 + j)

    def prepare(part):
        columns = slice(part * width, (part + 1) * width)
        sums[:, columns] = dot(jnp.ones((16, rows), bf16), dqkv[columns], 1, 1)[:8]
        if part == 0:
            gain_wide[...] = jnp.broadcast_to(vec_ref[0:1], (128, width)).T
            shift_wide[...] = jnp.broadcast_to(vec_ref[1:2], (128, width)).T
            small_wide[...] = jnp.zeros((width, 128), f32)
        if part == 2:
            lines = [jnp.zeros((2, width), f32), sums[0:1, :width], sums[0:1, 2 * width :]]
            lines += [jnp.sum(gvec_ref[i], axis=0, keepdims=True) for i in range(5)]
            lines.append(jnp.zeros((128 - VECTORS, width), f32))
            small_wide[...] += jnp.concatenate(lines, axis=0).T

    def weight_grad(j, part):
        lines = pl.ds(pl.multiple_of(j * level_rows, level_rows), level_rows)
        columns = pl.ds(pl.multiple_of(part * width, width), width)
        product = dot(unit_t[lines], dqkv[columns], 1, 1)
        weight = fq[lines, columns].astype(f32)
        line = sums[0:1, columns]
        gain_sum = jnp.sum(weight * product, axis=1, keepdims=True)
        shift_sum = jnp.sum(weight * line, axis=1, keepdims=True)
        lane = lax.broadcasted_iota(jnp.int32, (level_rows, 128), 1)
        small_wide[lines] += jnp.where(
            lane == 0, gain_sum, jnp.where(lane == 1, shift_sum, 0.0)
        )
        gain = jnp.concatenate([gain_wide[lines]] * (width // 128), axis=1)
        shift = jnp.concatenate([shift_wide[lines]] * (width // 128), axis=1)
        result[:, columns] = gain * product + shift * line

        @pl.when(part == 2)
        def _():
            small = small_wide[lines]
            blank = jnp.zeros((SHARD, 128), f32)
            for i in range(8):
                p = (i % 2) * CHIPS + 4 * j + i // 2
                some = slice(SHARD * i, SHARD * (i + 1))
                top = jnp.concatenate([result[some, :half_q], small[some]], axis=1)
                bottom = jnp.concatenate([result[some, half_q:], blank], axis=1)
                sq[p] = jnp.concatenate([top, bottom], axis=0).astype(bf16)

    def grad_rows(m):
        return pl.ds(pl.multiple_of(m * block, block), block)

    def grad_copy(m):
        return pltpu.make_async_copy(
            grad.at[grad_rows(m)], grad_hbm.at[grad_rows(m)], copy_sem.at[11 + shared + m]
        )

    def input_grad(m):
        some = grad_rows(m)
        d_normed = dot(fq[...], dqkv[:, some], 1, 0).T
        unit, factor = normalize(tok[some].astype(f32))
        share = norm_backward(d_normed, vec_ref[0:1], unit, factor)
        grad[some] = (dmix[some] + share).astype(bf16)

        @pl.when(m < shared)
        def _():
            grad_copy(m).start()

        @pl.when(m >= shared)
        def _():
            swap_copy(grad.at[some], grad_out.at[grad_rows(m - shared)], 0).start()

    def late_wait():
        for copy in late:
            copy.wait()

    sr_in.wait()
    at.await_all()
    sib_send(2, 2)
    sib_send(2, 1)
    sib_send(2, 0)
    sib_add(2, 2)
    sib_send(2, 3)
    sib_add(2, 1)
    unit_in.wait()
    part_wait(0)
    prepare(0)
    sib_add(2, 0)
    part_wait(1)
    sib_add(2, 3)
    prepare(1)

    def beside_weight_0():
        part_wait(2)
        prepare(2)

    def beside_weight_2():
        sib_send(1, 0)

    def beside_weight_4():
        corner_add(2, 0)
        corner_add(2, 1)
        sib_send(0, 0)

    def beside_weight_5():
        sib_send(0, 3)
        corner_add(2, 3)

    def beside_weight_6():
        corner_add(2, 2)

    def beside_weight_7():
        sib_add(0, 0)
        sib_add(0, 3)
        plane_add(2, 0)

    def beside_weight_8():
        sib_send(0, 1)
        sib_add(1, 0)
        plane_add(2, 3)

    def beside_weight_9():
        sib_add(0, 1)

    def beside_weight_10():
        corner_add(0, 3)
        sib_send(1, 3)


    def beside_weight_step(i, carry):
        turn = i // 3
        j = jnp.where(turn == 0, 0, jnp.where(turn == 1, 3, jnp.where(turn == 2, 1, 2)))
        weight_grad(j, lax.rem(i, 3))
        pl.when(i == 0)(beside_weight_0)
        pl.when(i == 2)(beside_weight_2)
        pl.when(i == 4)(beside_weight_4)
        pl.when(i == 5)(beside_weight_5)
        pl.when(i == 6)(beside_weight_6)
        pl.when(i == 7)(beside_weight_7)
        pl.when(i == 8)(beside_weight_8)
        pl.when(i == 9)(beside_weight_9)
        pl.when(i == 10)(beside_weight_10)
        return carry

    lax.fori_loop(0, 12, beside_weight_step, 0)
    corner_add(0, 0)
    sib_send(1, 2)
    plane_add(2, 2)
    sib_send(0, 2)
    corner_add(0, 1)
    plane_add(2, 1)
    sib_add(1, 3)
    sib_send(1, 1)
    mixed_in.wait()
    swap_copy(mixed, mixed_out, 1).start()
    late_wait()
    sib_add(1, 2)
    plane_add(0, 3)
    corner_add(1, 0)
    sib_add(0, 2)

    def beside_input_0():
        plane_add(0, 0)
        corner_add(1, 3)
        corner_add(1, 2)
        sib_add(1, 1)
        plane_add(0, 1)

    def beside_input_1():
        corner_add(0, 2)
        plane_add(1, 2)
        plane_add(1, 0)

    def beside_input_2():
        corner_add(1, 1)
        plane_add(1, 3)

    def beside_input_4():
        plane_add(0, 2)
        plane_add(1, 1)

    def beside_input_6():
        land(2)


    def beside_input_step(i, carry):
        input_grad(i)
        pl.when(i == 0)(beside_input_0)
        pl.when(i == 1)(beside_input_1)
        pl.when(i == 2)(beside_input_2)
        pl.when(i == 4)(beside_input_4)
        pl.when(i == 6)(beside_input_6)
        return carry

    lax.fori_loop(0, 8, beside_input_step, 0)
    land(0)
    land(1)
    for k in range(len(slabs)):
        every = cut(slabs[k][0], k, 0, DEVICES - 1)
        remote(k, every, every, at.sib, 0).wait_send()
    for m in range(shared):
        grad_copy(m).wait()
    swap_copy(grad.at[rows_of(shared, shared)], grad_out, 0).wait()
    swap_copy(mixed, mixed_out, 1).wait()


def scatter(packed, dqkv, unit_t, full_qkv, tokens, odd_tokens, d_mixed, mixed, vectors, sums):
    rows, width = tokens.shape
    wide = 3 * width
    vmem = pl.BlockSpec(memory_space=pltpu.VMEM)
    anywhere = pl.BlockSpec(memory_space=pl.ANY)
    tall = 2 * SHARD
    widths = (wide // 2 + 128, wide // 2)
    return pl.pallas_call(
        scatter_kernel,
        out_shape=[jax.ShapeDtypeStruct((rows // 2, width), bf16)] * 3
        + [jax.ShapeDtypeStruct((tall, w), f32) for w in widths],
        in_specs=[anywhere] * 8 + [vmem] * 2,
        out_specs=[anywhere] * 3 + [vmem] * 2,
        scratch_shapes=[pltpu.VMEM((DEVICES, tall, w), bf16) for w in widths]
        + [pltpu.VMEM((CHIPS, tall, w), bf16) for w in widths]
        + [pltpu.VMEM((4 * PLANES, tall, w), bf16) for w in widths]
        + [
            pltpu.VMEM((wide, rows), bf16),
            pltpu.VMEM((width, rows), bf16),
            pltpu.VMEM((width, wide), bf16),
            pltpu.VMEM((rows, width), bf16),
            pltpu.VMEM((rows, width), f32),
            pltpu.VMEM((rows, width), bf16),
            pltpu.VMEM((rows // 2, width), bf16),
            pltpu.VMEM((width, 128), f32),
            pltpu.VMEM((width, 128), f32),
            pltpu.VMEM((width, 128), f32),
            pltpu.VMEM((8, wide), f32),
            pltpu.VMEM((8 * SHARD, wide), f32),
            pltpu.SemaphoreType.DMA((3,)),
            pltpu.SemaphoreType.DMA((3, 5 * PLANES)),
            pltpu.SemaphoreType.DMA((2,)),
            pltpu.SemaphoreType.DMA((2,)),
            pltpu.SemaphoreType.DMA((19,)),
        ],
        compiler_params=pltpu.CompilerParams(
            collective_id=1, has_side_effects=True, vmem_limit_bytes=60 * MIB
        ),
    )(packed, dqkv, unit_t, full_qkv, tokens, odd_tokens, d_mixed, mixed, vectors, sums)


def finish_kernel(
    _, mixed_odd, grad_even, grad_odd, q_ref, r_ref, mixed, grad, g_qkv, g_out, g_in, g_back, *lines
):
    block = mixed_odd.shape[0]
    mixed[...] = mixed_odd[...]
    grad[:block] = grad_even[...]
    grad[block:] = grad_odd[...]

    @pl.when(pl.program_id(0) == 0)
    def _():
        width = g_out.shape[1]
        half_q = 3 * width // 2
        half = width // 2
        g_qkv[:, :half_q] = q_ref[:SHARD, :half_q]
        g_qkv[:, half_q:] = q_ref[SHARD:, :half_q]
        g_out[...] = r_ref[:SHARD, :width]
        g_in[...] = r_ref[SHARD:, :width]
        g_back[:, :half] = r_ref[:SHARD, width:]
        g_back[:, half:] = r_ref[SHARD:, width:]
        small = q_ref[:SHARD, half_q:].T
        for i, line in enumerate(lines):
            line[...] = small[i, :SHARD]


def finish(mixed, mixed_odd, grad, grad_odd, q_part, r_part, slots):
    rows, width = mixed.shape
    block = rows // slots
    single = pl.BlockSpec((block, width), lambda i: (i, 0))
    double = pl.BlockSpec((2 * block, width), lambda i: (i, 0))

    def whole(shape):
        return pl.BlockSpec(shape, lambda i: (0,) * len(shape))

    shapes = [(SHARD, 3 * width)] + [(SHARD, width)] * 3 + [(SHARD,)] * 9
    return pl.pallas_call(
        finish_kernel,
        grid=(slots // 2,),
        out_shape=[jax.ShapeDtypeStruct((rows, width), bf16)] * 2
        + [jax.ShapeDtypeStruct(s, f32) for s in shapes],
        in_specs=[pl.BlockSpec(memory_space=pl.ANY)]
        + [single] * 3
        + [whole(q_part.shape), whole(r_part.shape)],
        out_specs=[pl.BlockSpec((block, width), lambda i: (2 * i + 1, 0)), double]
        + [whole(s) for s in shapes],
        input_output_aliases={0: 0},
    )(mixed, mixed_odd, grad, grad_odd, q_part, r_part)


def on_one_plan(tokens, mol_len, cotangent, vectors, w_qkv, w_out, w_in, w_back):
    slots = mol_len.shape[0]
    (
        qkv,
        unit_t,
        full_qkv,
        full_out,
        full_in,
        full_back,
        odd_tokens,
        odd_cotangent,
        lines,
        lengths,
    ) = gather_and_project(mol_len, vectors, w_qkv, w_out, w_in, w_back, tokens, cotangent)
    mixed, d_mixed, dqkv, sums, mixed_sent, packed = middle(
        lengths,
        qkv,
        (tokens, odd_tokens),
        (cotangent, odd_cotangent),
        full_out,
        full_in,
        full_back,
        lines,
        True,
    )
    grad, grad_odd, mixed_odd, q_part, r_part = scatter(
        packed, dqkv, unit_t, full_qkv, tokens, odd_tokens, d_mixed, mixed_sent, lines, sums
    )
    mixed_out, token_grad, g_qkv, g_out, g_in, g_back, *small = finish(
        mixed, mixed_odd, grad, grad_odd, q_part, r_part, slots
    )
    return mixed_out, token_grad, small, g_qkv, g_out, g_in, g_back


def on_any_plan(tokens, mol_len, cotangent, vectors, w_qkv, w_out, w_in, w_back):
    slots = mol_len.shape[0]
    rows, width = tokens.shape

    def gather(array, axis):
        return lax.all_gather(array, "fsdp", axis=axis, tiled=True)

    lines = gather(jnp.stack(vectors), 1).astype(f32)
    lines = jnp.pad(lines, ((0, 16 - len(vectors)), (0, 0)))
    full_qkv, full_out, full_in, full_back = (
        gather(w, 0) for w in (w_qkv, w_out, w_in, w_back)
    )
    unit, factor = normalize(tokens.astype(f32))
    normed = (unit * lines[0] + lines[1]).astype(bf16)
    qkv = jnp.dot(normed, full_qkv, preferred_element_type=f32)
    qkv = (qkv + jnp.concatenate([lines[2], jnp.zeros_like(lines[2]), lines[3]])).astype(bf16)
    qkv = qkv.reshape(slots, rows // slots, 3 * width).transpose(0, 2, 1)
    mixed_out, d_mixed, dqkv, sums, g_out, g_in, g_back = middle(
        jnp.broadcast_to(mol_len[:, None], (slots, 128)),
        qkv,
        (tokens, tokens),
        (cotangent, cotangent),
        full_out,
        full_in,
        full_back,
        lines,
        False,
    )
    g_qkv = jnp.einsum("rf,dr->fd", normed, dqkv, preferred_element_type=f32)
    d_normed = jnp.einsum("dr,fd->rf", dqkv, full_qkv, preferred_element_type=f32)
    totals = jnp.sum(dqkv.astype(f32), axis=1)
    small = [jnp.sum(d_normed * unit, axis=0), jnp.sum(d_normed, axis=0)]
    small += [totals[:width], totals[2 * width :]]
    small += [jnp.sum(sums[i], axis=0) for i in range(5)]
    share = norm_backward(d_normed, lines[0], unit, factor)
    token_grad = (d_mixed + share).astype(bf16)

    def scatter_sum(array, axis):
        return lax.psum_scatter(array, "fsdp", scatter_dimension=axis, tiled=True)

    small = scatter_sum(jnp.stack(small), 1)
    return (
        mixed_out,
        token_grad,
        [small[i] for i in range(9)],
        *(scatter_sum(g, 0) for g in (g_qkv, g_out, g_in, g_back)),
    )


def per_device(
    devices,
    tokens,
    mol_len,
    cotangent,
    ln1_gain,
    ln1_bias,
    w_qkv,
    q_bias,
    v_bias,
    w_out,
    out_bias,
    ln2_gain,
    ln2_bias,
    w_in,
    in_bias,
    w_back,
    back_bias,
):
    vectors = [
        ln1_gain,
        ln1_bias,
        q_bias,
        v_bias,
        out_bias,
        ln2_gain,
        ln2_bias,
        in_bias,
        back_bias,
    ]
    known = devices == DEVICES and w_qkv.shape[0] == SHARD
    plan = on_one_plan if known else on_any_plan
    mixed_out, token_grad, small, g_qkv, g_out, g_in, g_back = plan(
        tokens, mol_len, cotangent, vectors, w_qkv, w_out, w_in, w_back
    )
    return (
        mixed_out,
        token_grad,
        small[0],
        small[1],
        g_qkv,
        small[2],
        small[3],
        g_out,
        small[4],
        small[5],
        small[6],
        g_in,
        small[7],
        g_back,
        small[8],
    )


def solution(mesh):
    line, matrix = P("fsdp"), P("fsdp", None)
    return jax.shard_map(
        functools.partial(per_device, mesh.shape["fsdp"]),
        mesh=mesh,
        in_specs=(
            matrix,
            line,
            matrix,
            line,
            line,
            matrix,
            line,
            line,
            matrix,
            line,
            line,
            line,
            matrix,
            line,
            matrix,
            line,
        ),
        out_specs=(
            matrix,
            matrix,
            line,
            line,
            matrix,
            line,
            line,
            matrix,
            line,
            line,
            line,
            matrix,
            line,
            matrix,
            line,
        ),
        check_vma=False,
    )
```

profile of v0, /device:TPU:0, one launch (start us, length us, event | category | flops | bytes accessed | tf_op | source)
XLA Modules:
  0.0 171.2 jit_solution(3711175196498252788)
XLA Ops:
  0.7 53.3 %shard_map.271 = (bf16[8,2304,256]{2,1,0:T(8,128)(2,1)}, bf16[768,2048]{1,0:T(8,128)(2,1)}, bf16[768,2304]{1,0:T(8,128)(2,1)}, bf16[768,768]{1,0:T(8,128)(2,1)},...) custom-call(s32[8]{0:T(128)} %len_ref.1, ...), custom_call_target="tpu_custom_call" | custom-call | tf_op jit(solution)/shard_map/pallas_call | solution.py:489
  54.0 37.6 %shard_map.272 = (bf16[2048,768]{1,0:T(8,128)(2,1)}, f32[2048,768]{1,0:T(8,128)}, bf16[2304,2048]{1,0:T(8,128)(2,1)}, f32[5,8,768]{2,1,0:T(8,128)}, bf16[1024,76...) custom-call(s32[8,128]{1,0:T(8,128)} %get-tuple-element.51.len_ref, bf16[8,2304,256]{2,1,0:T(8,128)(2,1)} %get-tuple-element.52.qkv_ref, ...), custom_call_target="tpu_custom_call" | custom-call | tf_op jit(solution)/shard_map/pallas_call | solution.py:885
  91.6 73.9 %shard_map.273 = (bf16[1024,768]{1,0:T(8,128)(2,1)}, bf16[1024,768]{1,0:T(8,128)(2,1)}, bf16[1024,768]{1,0:T(8,128)(2,1)}, f32[48,1280]{1,0:T(8,128)}, f32[48,1152]{1,0:T(8,128)}) custom-call(bf16[32,48,1152]{2,1,0:T(8,128)(2,1)} %get-tuple-element.60.sr_hbm, bf16[2304,2048]{1,0:T(8,128)(2,1)} %get-tuple-element.61.dqkv_hbm, ...), custom_call_target="tpu_custom_call" | custom-call | tf_op jit(solution)/shard_map/pallas_call | solution.py:1295
  165.5 5.5 %shard_map.274 = (bf16[2048,768]{1,0:T(8,128)(2,1)}, bf16[2048,768]{1,0:T(8,128)(2,1)}, f32[24,2304]{1,0:T(8,128)}, f32[24,768]{1,0:T(8,128)}, f32[24,768]{1,0:T...) custom-call(bf16[2048,768]{1,0:T(8,128)(2,1)} %get-tuple-element.59., ...), custom_call_target="tpu_custom_call", output_to_operand_aliasing={{0}: (0, {})} | custom-call | tf_op jit(solution)/shard_map/pallas_call | solution.py:1363
where the time goes:
time: 172 us; the launch traced here: 171 us
  Pallas kernels  170 us (99%)
    pallas_call x1, Pallas kernels, scatter(): pl.pallas_call(scatter_kernel, out_shape=[jax.ShapeDtypeStruct((rows // 2...  73.9 us
    pallas_call x1, Pallas kernels, gather_and_project(): pl.pallas_call(gather_kernel, out_shape=[jax.ShapeDtypeStruct((slots, wid...  53.3 us
    pallas_call x1, Pallas kernels, middle(): pl.pallas_call(functools.partial(middle_kernel, packed, width // HEADS),...  37.6 us
    pallas_call x1, Pallas kernels, finish(): pl.pallas_call(finish_kernel, grid=(slots // 2,), out_shape=[jax.ShapeDty...  5.5 us

commit v1 on v0

--- a/solution.py
+++ b/solution.py
@@ -93,7 +93,7 @@
     wo_ref,
     wi_ref,
     wb_ref,
-    tok_ref,
+    tok_in,
     cot_hbm,
     qkv_hbm,
     unit_hbm,
@@ -116,6 +116,7 @@
     unit_t,
     qkv,
     bias,
+    tok_ref,
     tok_odd,
     cot_odd,
     len_send,
@@ -124,12 +125,21 @@
     recv_sem,
     swap_send,
     swap_recv,
+    slot_sem,
     copy_sem,
 ):
     at = Place()
     at.greet()
     width = tok_ref.shape[1]
     slots, _, block = qkv.shape
+    slot_in = [
+        pltpu.make_async_copy(
+            tok_in.at[pl.ds(i * block, block)], tok_ref.at[pl.ds(i * block, block)], slot_sem.at[i]
+        )
+        for i in range(slots)
+    ]
+    for i in [0, 2] + list(range(1, slots, 2)) + list(range(4, slots, 2)):
+        slot_in[i].start()
     shared = slots // 2
     half_q = 3 * width // 2
     half = width // 2
@@ -259,6 +269,7 @@
     def swap_start():
         swap_copy(len_send, len_recv, 2, 5).start()
         for i in range(shared):
+            slot_in[2 * i + 1].wait()
             tok_copy(i).start()
         for i in range(shared):
             cot_in[i].wait()
@@ -285,6 +296,7 @@
     def norm_step(m):
         rows = rows_of(m)
         if m < shared:
+            slot_in[2 * m].wait()
             here = tok_ref[rows_of(2 * m)]
         else:
             tok_copy(m - shared).wait_recv()
@@ -371,7 +383,6 @@
     norm_step(0)
     norm_step(1)
     at.await_all()
-    swap_start()
     own_column(0)
     own_column(1)
     own_plane(1)
@@ -379,6 +390,7 @@
     norm_step(2)
     own_plane(4)
     own_plane(3)
+    swap_start()
     own_column(2)
     own_plane(0)
     column(0, 3)
@@ -500,7 +512,7 @@
             jax.ShapeDtypeStruct((16, width), f32),
             jax.ShapeDtypeStruct((slots, 128), jnp.int32),
         ],
-        in_specs=[pl.BlockSpec(memory_space=pltpu.SMEM)] + [vmem] * (VECTORS + 5) + [anywhere],
+        in_specs=[pl.BlockSpec(memory_space=pltpu.SMEM)] + [vmem] * (VECTORS + 4) + [anywhere] * 2,
         out_specs=[anywhere] * 8 + [vmem] * 2,
         scratch_shapes=[
             pltpu.VMEM((DEVICES, 2 * SHARD, wide // 2 + 128), bf16),
@@ -514,6 +526,7 @@
             pltpu.VMEM((width, rows), bf16),
             pltpu.VMEM((slots, wide, block), bf16),
             pltpu.VMEM((wide, 128), f32),
+            pltpu.VMEM((rows, width), bf16),
             pltpu.VMEM((rows // 2, width), bf16),
             pltpu.VMEM((rows // 2, width), bf16),
             pltpu.VMEM((slots, 128), jnp.int32),
@@ -522,6 +535,7 @@
             pltpu.SemaphoreType.DMA((5, CHIPS + 1)),
             pltpu.SemaphoreType.DMA((3,)),
             pltpu.SemaphoreType.DMA((6 + slots // 2,)),
+            pltpu.SemaphoreType.DMA((slots,)),
             pltpu.SemaphoreType.DMA((COPIES + slots,)),
         ],
         compiler_params=pltpu.CompilerParams(
@@ -539,9 +553,9 @@
     tok_second,
     cot_first,
     cot_second,
-    wout_ref,
-    win_ref,
-    wback_ref,
+    wout_hbm,
+    win_hbm,
+    wback_hbm,
     vec_ref,
     mixed_out,
     dmix_ref,
@@ -553,7 +567,8 @@
         mixed_odd, packed_ref, gout_ref, gin_ref, gback_ref, *rest = rest
     else:
         gout_ref, gin_ref, gback_ref, *rest = rest
-    probs, ctx_s, linv_s, dctx_s, tok_ref, cot_ref, mixed_ref = rest
+    probs, ctx_s, linv_s, dctx_s, tok_ref, cot_ref, mixed_ref, *rest = rest
+    wout_ref, win_ref, wback_ref, weight_sem = rest
     step = pl.program_id(0)
     block, width = tok_ref.shape
     slot = 32
@@ -566,8 +581,21 @@
     tok_ref[...] = jnp.where(first, tok_first[...], tok_second[...])
     cot_ref[...] = jnp.where(first, cot_first[...], cot_second[...])
 
+    weight_copies = [
+        pltpu.make_async_copy(src, dst, weight_sem.at[i])
+        for i, (src, dst) in enumerate(
+            ((wout_hbm, wout_ref), (win_hbm, win_ref), (wback_hbm, wback_ref))
+        )
+    ]
+
+    def await_weights():
+        for copy in weight_copies:
+            copy.wait()
+
     @pl.when(step == 0)
     def _():
+        for copy in weight_copies:
+            copy.start()
         gout_ref[...] = jnp.zeros_like(gout_ref)
         gin_ref[...] = jnp.zeros_like(gin_ref)
         gback_ref[...] = jnp.zeros_like(gback_ref)
@@ -658,6 +686,7 @@
 
         forward()
 
+        pl.when(step == 0)(await_weights)
         live = (lax.broadcasted_iota(jnp.int32, (keys, 1), 0) < length).astype(f32)
         out_bias, gain, shift = vec_ref[4:5], vec_ref[5:6], vec_ref[6:7]
         in_bias, back_bias = vec_ref[7:8], vec_ref[8:9]
@@ -789,6 +818,8 @@
 
     half = block // 2
 
+    pl.when((step == 0) & (length == 0))(await_weights)
+
     @pl.when(length == 0)
     def _():
         mixed_ref[...] = tok_ref[...]
@@ -882,6 +913,7 @@
     else:
         out_specs += [whole(square)] * 3
         out_shape += [jax.ShapeDtypeStruct(square, f32)] * 3
+    scratch += [pltpu.VMEM(square, bf16)] * 3 + [pltpu.SemaphoreType.DMA((3,))]
     return pl.pallas_call(
         functools.partial(middle_kernel, packed, width // HEADS),
         grid=(slots,),
@@ -892,9 +924,9 @@
             second,
             first,
             second,
-            whole(square),
-            whole(square),
-            whole(square),
+            pl.BlockSpec(memory_space=pl.ANY),
+            pl.BlockSpec(memory_space=pl.ANY),
+            pl.BlockSpec(memory_space=pl.ANY),
             whole((16, width)),
         ],
         out_specs=out_specs,

time: 172 us -> 171 us (level); the launches traced: 171 us -> 172 us
    pallas_call x1, Pallas kernels: 37.6 us -> 45.5 us  [middle(): pl.pallas_call(functools.partial(middle_kernel, packed, width // HEADS),...]
    pallas_call x1, Pallas kernels: 73.9 us -> 68.6 us  [scatter(): pl.pallas_call(scatter_kernel, out_shape=[jax.ShapeDtypeStruct((rows // 2...]
where the time goes in v1:
time: 171 us; the launch traced here: 172 us
  Pallas kernels  171 us (100%)
    pallas_call x1, Pallas kernels, scatter(): pl.pallas_call(scatter_kernel, out_shape=[jax.ShapeDtypeStruct((rows // 2...  68.6 us
    pallas_call x1, Pallas kernels, gather_and_project(): pl.pallas_call(gather_kernel, out_shape=[jax.ShapeDtypeStruct((slots, wid...  51.6 us
    pallas_call x1, Pallas kernels, middle(): pl.pallas_call(functools.partial(middle_kernel, packed, width // HEADS),...  45.5 us
    pallas_call x1, Pallas kernels, finish(): pl.pallas_call(finish_kernel, grid=(slots // 2,), out_shape=[jax.ShapeDty...  5.5 us

profile of v1, /device:TPU:0, one launch (start us, length us, event | category | flops | bytes accessed | tf_op | source)
XLA Modules:
  0.0 172.1 jit_solution(11114861177460959454)
XLA Ops:
  0.7 51.6 %shard_map.271 = (bf16[8,2304,256]{2,1,0:T(8,128)(2,1)}, bf16[768,2048]{1,0:T(8,128)(2,1)}, bf16[768,2304]{1,0:T(8,128)(2,1)}, bf16[768,768]{1,0:T(8,128)(2,1)},...) custom-call(s32[8]{0:T(128)} %len_ref.1, ...), custom_call_target="tpu_custom_call" | custom-call | tf_op jit(solution)/shard_map/pallas_call | solution.py:501
  52.2 45.5 %shard_map.272 = (bf16[2048,768]{1,0:T(8,128)(2,1)}, f32[2048,768]{1,0:T(8,128)}, bf16[2304,2048]{1,0:T(8,128)(2,1)}, f32[5,8,768]{2,1,0:T(8,128)}, bf16[1024,76...) custom-call(s32[8,128]{1,0:T(8,128)} %get-tuple-element.51.len_ref, bf16[8,2304,256]{2,1,0:T(8,128)(2,1)} %get-tuple-element.52.qkv_ref, ...), custom_call_target="tpu_custom_call" | custom-call | tf_op jit(solution)/shard_map/pallas_call | solution.py:917
  97.8 68.6 %shard_map.273 = (bf16[1024,768]{1,0:T(8,128)(2,1)}, bf16[1024,768]{1,0:T(8,128)(2,1)}, bf16[1024,768]{1,0:T(8,128)(2,1)}, f32[48,1280]{1,0:T(8,128)}, f32[48,1152]{1,0:T(8,128)}) custom-call(bf16[32,48,1152]{2,1,0:T(8,128)(2,1)} %get-tuple-element.60.sr_hbm, bf16[2304,2048]{1,0:T(8,128)(2,1)} %get-tuple-element.61.dqkv_hbm, ...), custom_call_target="tpu_custom_call" | custom-call | tf_op jit(solution)/shard_map/pallas_call | solution.py:1327
  166.4 5.5 %shard_map.274 = (bf16[2048,768]{1,0:T(8,128)(2,1)}, bf16[2048,768]{1,0:T(8,128)(2,1)}, f32[24,2304]{1,0:T(8,128)}, f32[24,768]{1,0:T(8,128)}, f32[24,768]{1,0:T...) custom-call(bf16[2048,768]{1,0:T(8,128)(2,1)} %get-tuple-element.59., ...), custom_call_target="tpu_custom_call", output_to_operand_aliasing={{0}: (0, {})} | custom-call | tf_op jit(solution)/shard_map/pallas_call | solution.py:1395
